TPU v7x, 32 devices: a whole 2x2x4 slice. The times are simulated.
32 devices in a mesh: fsdp: 8 (over z, y), dp: 4 (over x, core).
Axes of the slice: x: 2, y: 2, z: 4, core: 2. Of those that a mesh axis runs over, the one named last changes fastest.
Arguments:
- patch_acts: bfloat16 [4096, 12288], P(('fsdp', 'dp')), may hold values from -6 to 6
- patch_slot: int32 [4096], P(('fsdp', 'dp')), may hold values from 0 to 256, as said below
- out_grads: bfloat16 [2048, 3072], P(('fsdp', 'dp')), may hold values from -6 to 6
- latent_weight: bfloat16 [12288, 3072], P('dp', 'fsdp'), may hold values from -0.0546875 to 0.0546875
- step_size: bfloat16 [1, 3072], P(None, 'fsdp')
Outputs:
- grad_acts: bfloat16 [4096, 12288], P(('fsdp', 'dp'))
- grad_weight: float32 [12288, 3072], P('dp', 'fsdp')
- grad_step: float32 [1, 3072], P(None, 'fsdp')
Inputs may be any that keep to these rules, and one draw needn't show every extreme that they name: `patch_slot`: within each fsdp index, the used patch rows of every image owner come first in its 128 slots and carry a packed row below 256, the others carry 256; each packed row of the fsdp index receives exactly one patch row; in every fsdp index some image owner has all 128 slots used.
All inputs are finite; a program needn't handle non-finite values.
Results may differ from a plain program's by a relative error of at most 0.0049.
Values may be sent and summed in bfloat16 or wider, within the bound.
A program may use at most 128 MiB of HBM per device.

v0:
```python
import jax
import jax.numpy as jnp
from jax import lax
from jax.sharding import PartitionSpec as P

FF_W = 12288


top_level = 7.0
wobble = 0.9
two_pi = 6.283185307179586
inv_root_two = 0.7071067811865476
inv_root_tau = 0.3989422804014327


def gelu_pair(values):
    normal_cdf = 0.5 * (1.0 + jax.scipy.special.erf(values * inv_root_two))
    density = jnp.exp(-0.5 * values * values) * inv_root_tau
    return (values * normal_cdf, normal_cdf + values * density)


def soft_quantize(weight, step):
    ratio = weight / step
    clipped = top_level * jnp.tanh(ratio / top_level)
    phase = two_pi * clipped
    quantized = clipped - wobble * jnp.sin(phase) / two_pi
    slope = (1.0 - wobble * jnp.cos(phase)) * (1.0 - clipped / top_level * (clipped / top_level))
    return (quantized, slope, ratio)


def contract_last(left, right):
    return lax.dot_general(
        left, right, (((1,), (1,)), ((), ())), preferred_element_type=jnp.float32
    )


def contract_first(left, right):
    return lax.dot_general(
        left, right, (((0,), (0,)), ((), ())), preferred_element_type=jnp.float32
    )


def shards(patch_acts, patch_slot, out_grads, latent_weight, step_size):
    dp_count = lax.axis_size("dp")
    capacity, features = patch_acts.shape
    hidden = features // dp_count
    packed_rows = out_grads.shape[0] * dp_count
    outgoing = patch_acts.reshape(capacity, dp_count, hidden)
    labels = jnp.broadcast_to(patch_slot[:, None], (capacity, dp_count))
    incoming, slot_labels = (
        lax.all_to_all(outgoing, "dp", split_axis=1, concat_axis=0, tiled=True),
        lax.all_to_all(labels, "dp", split_axis=1, concat_axis=0, tiled=True),
    )
    incoming = incoming.reshape(dp_count * capacity, hidden)
    slot_labels = slot_labels.reshape(dp_count * capacity)
    holder = jnp.zeros((packed_rows + 1, hidden), jnp.bfloat16).at[slot_labels].set(incoming)
    packed = holder[:packed_rows]
    act_full, gelu_slope = gelu_pair(packed.astype(jnp.float32))
    act = act_full.astype(jnp.bfloat16)
    full_grads = lax.all_gather(out_grads, "dp", axis=0, tiled=True)
    step_local = step_size.astype(jnp.float32)
    quantized, slope, ratio = soft_quantize(latent_weight.astype(jnp.float32), step_local)
    step_piece = lax.all_gather(step_size, "fsdp", axis=1, tiled=True).astype(jnp.float32)
    piece_quant, piece_slope, piece_ratio = soft_quantize(
        lax.all_gather(latent_weight, "fsdp", axis=1, tiled=True).astype(jnp.float32), step_piece
    )
    piece_weight = (step_piece * piece_quant).astype(jnp.bfloat16)
    columns = full_grads
    grad_hidden = contract_last(columns, piece_weight)
    grad_packed = (grad_hidden * gelu_slope).astype(jnp.bfloat16)
    padded = jnp.concatenate([grad_packed, jnp.zeros((1, hidden), jnp.bfloat16)], axis=0)
    picked = jnp.take(padded, slot_labels, axis=0).reshape(dp_count * capacity, 1, hidden)
    returned = lax.all_to_all(picked, "dp", split_axis=0, concat_axis=1, tiled=True)
    grad_acts = returned.reshape(capacity, features)
    columns = full_grads
    grad_qweight = lax.psum_scatter(
        contract_first(columns, act), "fsdp", scatter_dimension=0, tiled=True
    ).T
    grad_weight = grad_qweight * slope
    partial_step = jnp.sum(grad_qweight * (quantized - ratio * slope), axis=0, keepdims=True)
    scale_factor = (FF_W * top_level) ** (-0.5)
    grad_step = scale_factor * lax.psum(partial_step, "dp")
    return (grad_acts, grad_weight, grad_step)


def solution(mesh):
    return jax.shard_map(
        shards,
        mesh=mesh,
        in_specs=(
            P(("fsdp", "dp"), None),
            P(("fsdp", "dp")),
            P(("fsdp", "dp"), None),
            P("dp", "fsdp"),
            P(None, "fsdp"),
        ),
        out_specs=(P(("fsdp", "dp"), None), P("dp", "fsdp"), P(None, "fsdp")),
        check_vma=False,
    )
```

profile of v0, /device:TPU:1, one launch (start us, length us, event | category | flops | bytes accessed | tf_op | source)
XLA Modules:
  0.0 1043.4 jit_solution(12695761160720270632)
XLA Ops:
  8.6 1.2 broadcast_in_dim.24
  9.9 4.3 all-to-all-start
  14.1 3.8 copy.24
  18.0 3.7 all-to-all-start.1
  21.7 42.0 %all-to-all-done.1 = bf16[128,4,3072]{2,0,1:T(8,128)(2,1)S(1)} async-done(((bf16[128,4,3072]{2,0,1:T(8,128)(2,1)}), bf16[128,4,3072]{2,0,1:T(8,128)(2,1)S(1)}, u32[]{:S(2)}, u32[]{:S(2)}) %all-to-all-start.1) | async-done | bytes 3145760 | tf_op jit(solution)/shard_map/all_to_all | solution.py:51
  63.7 1.7 copy-done
  65.4 6.5 scatter_custom_fusion
  71.9 16.5 %convolution_bitcast_fusion = f32[3072,3072]{0,1:T(8,128)} fusion(bf16[256,3072]{1,0:T(8,128)(2,1)} %all-gather.5.cloned.1.call-done, bf16[257,3072]{1,0:T(8,128)(2,1)S(1)} %scatter_custom_fusion), kind=kOutput, calls=%fused_computation.3 | convolution fusion | flops 4836556800 | bytes 40894464 | tf_op jit(solution)/shard_map/dot_general | solution.py:38
  89.1 25.3 %all_gather.9 = bf16[1,3072]{1,0:T(2,128)(2,1)S(1)} all-gather(bf16[1,384]{1,0:T(2,128)(2,1)S(1)} %copy-done.2), channel_id=1, replica_groups=mesh['fsdp'=8,'dp'=4] {'fsdp'}, dimensions={1}, use_global_device_ids=true | all-gather | bytes 6912 | tf_op jit(solution)/shard_map/all_gather | solution.py:63
  114.4 286.4 %all-gather.3.cloned.1.call-done = bf16[3072,3072]{1,0:T(8,128)(2,1)} async-done(((bf16[3072,384]{1,0:T(8,128)(2,1)}), bf16[3072,3072]{1,0:T(8,128)(2,1)}) %all-gather.3.cloned.1.call-update) | async-done | bytes 18874384 | tf_op jit(solution)/shard_map/all_gather | solution.py:65
  400.8 144.4 %fusion.5 = bf16[256,3072]{1,0:T(8,128)(2,1)S(1)} fusion(bf16[256,3072]{1,0:T(8,128)(2,1)S(1)} %copy-done.1, bf16[3072,3072]{1,0:T(8,128)(2,1)} %all-gather.3.cloned.1.call-done, f32[3072]{0:T(1024)S(1)} %bitcast.45, bf16[257,3072]{1,0:T(8,128)(2,1)S(1)} %scatter_custom_fusion), kind=kOutput, calls=%fused_computation.19 | convolution fusion | flops 4925423616 | bytes 23605248 | tf_op jit(solution)/shard_map/dot_general | solution.py:32
  545.4 3.8 gather_fusion
  549.2 2.3 bitcast_select_fusion
  552.0 3.8 reduce.2
  555.8 5.2 reshape.115
  561.0 4.3 all-to-all-start.2
  565.4 36.2 %all-to-all-done.2 = bf16[4,2,196608]{2,1,0:T(2,128)(2,1)S(1)} async-done(((bf16[4,2,196608]{2,1,0:T(2,128)(2,1)}), bf16[4,2,196608]{2,1,0:T(2,128)(2,1)S(1)}, u32[]{:S(2)}, u32[]{:S(2)}) %all-to-all-start.2) | async-done | bytes 3145760 | tf_op jit(solution)/shard_map/all_to_all | solution.py:73
  601.5 4.3 reshape.116
  605.9 5.6 copy.21
  611.4 3.5 copy.19
  614.9 2.8 copy.20
  617.7 391.1 %reduce-scatter.2.cloned.1.call-done = f32[384,3072]{0,1:T(8,128)} async-done(((f32[3072,3072]{0,1:T(8,128)}), f32[384,3072]{0,1:T(8,128)}) %reduce-scatter.2.cloned.1.call-update) | async-done | bytes 4718608 | tf_op jit(solution)/shard_map/reduce_scatter | solution.py:76
  1008.8 21.8 %fusion.1 = (f32[384]{0:T(512)S(1)}, f32[3072,384]{1,0:T(8,128)}) fusion(f32[384,3072]{0,1:T(8,128)} %reduce-scatter.2.cloned.1.call-done, bf16[3072,384]{1,0:T(8,128)(2,1)} %param.8, f32[384]{0:T(512)S(1)} %convert_reduce_fusion), kind=kLoop, calls=%fused_computation.12 | loop fusion | flops 20053632 | bytes 11799552 | tf_op jit(solution)/shard_map/reduce_sum | solution.py:80
  1030.7 5.6 psum.7
  (22 shorter events, 3.5 us)
Async XLA Ops:
  7.2 64.8 %all-gather.5.cloned.1.call-start = ((), (), s32[]{:S(2)}) async-start(), calls=%async_computation.5 | async-start | bytes 1966080 | tf_op jit(solution)/shard_map/all_gather | solution.py:60
  7.9 392.9 %all-gather.3.cloned.1.call-start = ((), (), s32[]{:S(2)}) async-start(), calls=%async_computation.4 | async-start | bytes 21233664 | tf_op jit(solution)/shard_map/all_gather | solution.py:65
  9.9 8.1 all-to-all-start
  18.0 45.8 %all-to-all-start.1 = ((bf16[128,4,3072]{2,0,1:T(8,128)(2,1)}), bf16[128,4,3072]{2,0,1:T(8,128)(2,1)S(1)}, u32[]{:S(2)}, u32[]{:S(2)}) async-start(bf16[128,4,3072]{2,0,1:T(8,128)(2,1)} %bitcast.39), calls=%async_computation.1 | async-start | bytes 6291456 | tf_op jit(solution)/shard_map/all_to_all | solution.py:51
  21.7 987.2 %reduce-scatter.2.cloned.1.call-start = ((), (), s32[]{:S(2)}) async-start(), calls=%async_computation.6 | async-start | bytes 42467328 | tf_op jit(solution)/shard_map/reduce_scatter | solution.py:76
  63.7 1.7 copy-start
  88.4 0.7 copy-start.2
  88.4 312.4 %copy-start.1 = (bf16[256,3072]{1,0:T(8,128)(2,1)S(1)}, bf16[256,3072]{1,0:T(8,128)(2,1)}, u32[]{:S(2)}) copy-start(bf16[256,3072]{1,0:T(8,128)(2,1)} %all-gather.5.cloned.1.call-done) | copy-start | bytes 4718596
  561.0 40.5 %all-to-all-start.2 = ((bf16[4,2,196608]{2,1,0:T(2,128)(2,1)}), bf16[4,2,196608]{2,1,0:T(2,128)(2,1)S(1)}, u32[]{:S(2)}, u32[]{:S(2)}) async-start(bf16[4,2,196608]{2,1,0:T(2,128)(2,1)} %reshape.115), calls=%async_computation.2 | async-start | bytes 6291456 | tf_op jit(solution)/shard_map/all_to_all | solution.py:73
Sparse Core Ops, SparseCore 0:
  9.6 27.7 all-gather.4
  38.9 361.8 all-gather.2
  404.7 604.1 reduce-scatter.1
where the time goes:
time: 1050 us; the launch traced here: 1040 us
  waiting for transfers between devices  757 us (72%)
  matrix products  161 us (15%)
  local copies, waits for them, and re-layouts  39.8 us (4%)
  blocking collectives  30.9 us (3%)
  other arithmetic  28.5 us (3%)
  between operations  13.8 us (1%)
  starting transfers between devices  12.4 us (1%)
    reduce_scatter x1, waiting for transfers between devices, shards(): lax.psum_scatter(contract_first(columns, act), 'fsdp', scatter_dimension=...  391 us
    all_gather x1, waiting for transfers between devices, shards(): lax.all_gather(latent_weight, 'fsdp', axis=1, tiled=True)  286 us
    dot_general x1, matrix products, contract_last(): lax.dot_general(left, right, (((1,), (1,)), ((), ())), preferred_element_...  144 us
    all_to_all x1, waiting for transfers between devices, shards(): lax.all_to_all(outgoing, 'dp', split_axis=1, concat_axis=0, tiled=True)  42 us
    all_to_all x1, waiting for transfers between devices, shards(): lax.all_to_all(picked, 'dp', split_axis=0, concat_axis=1, tiled=True)  36.2 us
    all_gather x1, blocking collectives, shards(): lax.all_gather(step_size, 'fsdp', axis=1, tiled=True).astype(jnp.float32)  25.3 us
    reduce_sum x1, other arithmetic, shards(): jnp.sum(grad_qweight * (quantized - ratio * slope), axis=0, keepdims=True)  21.8 us
  transfers between devices with their start and end apart: 6, of which 4 were waited for; matrix products, arithmetic and copies ran while one was open for 20% of the time, Pallas kernels for 0%

commit v1 on v0

v1 whole, which is shorter than its diff:
```python
import jax
import jax.numpy as jnp
from jax import lax
from jax.sharding import PartitionSpec as P

FF_W = 12288


top_level = 7.0
wobble = 0.9
two_pi = 6.283185307179586
inv_root_two = 0.7071067811865476
inv_root_tau = 0.3989422804014327


def gelu_pair(values):
    normal_cdf = 0.5 * (1.0 + jax.scipy.special.erf(values * inv_root_two))
    density = jnp.exp(-0.5 * values * values) * inv_root_tau
    return (values * normal_cdf, normal_cdf + values * density)


def soft_quantize(weight, step):
    ratio = weight / step
    clipped = top_level * jnp.tanh(ratio / top_level)
    phase = two_pi * clipped
    quantized = clipped - wobble * jnp.sin(phase) / two_pi
    slope = (1.0 - wobble * jnp.cos(phase)) * (1.0 - clipped / top_level * (clipped / top_level))
    return (quantized, slope, ratio)


def contract(left, right, dims):
    return lax.dot_general(left, right, (dims, ((), ())), preferred_element_type=jnp.float32)


def shards(patch_acts, patch_slot, out_grads, latent_weight, step_size):
    dp_count = lax.axis_size("dp")
    fsdp_count = lax.axis_size("fsdp")
    line_count = fsdp_count // 2
    lines = [[2 * i + s for i in range(line_count)] for s in range(2)]
    swap = [(i, i ^ 1) for i in range(fsdp_count)]
    side = lax.rem(lax.axis_index("fsdp"), 2)
    capacity, features = patch_acts.shape
    hidden = features // dp_count
    own_rows, width = out_grads.shape
    packed_rows = own_rows * dp_count
    columns = width // fsdp_count

    grads = lax.all_to_all(
        out_grads.reshape(own_rows, line_count, 2 * columns), "fsdp",
        split_axis=1, concat_axis=0, tiled=True, axis_index_groups=lines,
    ).reshape(line_count * own_rows, 2 * columns)
    grads = lax.all_gather(grads, "dp", axis=0, tiled=False)
    grads = grads.reshape(dp_count, line_count, own_rows, 2 * columns).transpose(1, 0, 2, 3)
    grads = grads.reshape(line_count * packed_rows, 2 * columns)
    grads_own = lax.dynamic_slice_in_dim(grads, side * columns, columns, 1)
    grads_other = lax.dynamic_slice_in_dim(grads, (1 - side) * columns, columns, 1)

    outgoing = patch_acts.reshape(capacity, dp_count, hidden)
    incoming = lax.all_to_all(outgoing, "dp", split_axis=1, concat_axis=0, tiled=True)
    incoming = incoming.reshape(dp_count * capacity, hidden)
    slots = lax.all_gather(patch_slot, "dp", axis=0, tiled=True)
    place = (lax.broadcasted_iota(jnp.int32, (packed_rows, dp_count * capacity), 0) == slots[None, :])
    place = place.astype(jnp.bfloat16)

    step = step_size.astype(jnp.float32)
    quantized, slope, ratio = soft_quantize(latent_weight.astype(jnp.float32), step)
    weight_own = (step * quantized).astype(jnp.bfloat16)
    weight_other = lax.ppermute(weight_own, "fsdp", swap)

    packed = contract(place, incoming, ((1,), (0,)))
    act_full, gelu_slope = gelu_pair(packed)
    act = act_full.astype(jnp.bfloat16)

    partial_hidden = contract(grads_own, weight_own, ((1,), (1,))) + contract(
        grads_other, weight_other, ((1,), (1,))
    )
    grad_hidden = lax.psum_scatter(
        partial_hidden.astype(jnp.bfloat16), "fsdp",
        scatter_dimension=0, tiled=True, axis_index_groups=lines,
    ).astype(jnp.float32)
    act_all = lax.all_gather(act, "fsdp", axis=0, tiled=True, axis_index_groups=lines)

    grad_packed = (grad_hidden * gelu_slope).astype(jnp.bfloat16)
    picked = contract(place, grad_packed, ((0,), (0,))).astype(jnp.bfloat16)
    returned = lax.all_to_all(
        picked.reshape(dp_count * capacity, 1, hidden), "dp", split_axis=0, concat_axis=1, tiled=True
    )
    grad_acts = returned.reshape(capacity, features)

    half_other = contract(act_all, grads_other, ((0,), (0,))).astype(jnp.bfloat16)
    half_arrived = lax.ppermute(half_other, "fsdp", swap).astype(jnp.float32)
    grad_qweight = contract(act_all, grads_own, ((0,), (0,))) + half_arrived
    grad_weight = grad_qweight * slope
    partial_step = jnp.sum(grad_qweight * (quantized - ratio * slope), axis=0, keepdims=True)
    scale_factor = (FF_W * top_level) ** (-0.5)
    grad_step = scale_factor * lax.psum(partial_step, "dp")
    return (grad_acts, grad_weight, grad_step)


def solution(mesh):
    return jax.shard_map(
        shards,
        mesh=mesh,
        in_specs=(
            P(("fsdp", "dp"), None),
            P(("fsdp", "dp")),
            P(("fsdp", "dp"), None),
            P("dp", "fsdp"),
            P(None, "fsdp"),
        ),
        out_specs=(P(("fsdp", "dp"), None), P("dp", "fsdp"), P(None, "fsdp")),
        check_vma=False,
    )
```

time: 1050 us -> 535 us (0.51)
  waiting for transfers between devices: 757 us -> 328 us
  matrix products: 161 us -> 51.5 us
  blocking collectives: 30.9 us -> 82.6 us
  other arithmetic: 28.5 us -> 5.61 us
    reduce_scatter x1, waiting for transfers between devices: 391 us -> 111 us  [shards(): lax.psum_scatter(partial_hidden.astype(jnp.bfloat16), 'fsdp', scatter_dim...]
    all_gather x2, waiting for transfers between devices: 286 us -> 112 us  [the longest x1 112 us: shards(): lax.all_gather(act, 'fsdp', axis=0, tiled=True, axis_index_groups=lines)]
    dot_general x2 -> x6, matrix products: 161 us -> 51.5 us  [contract(): lax.dot_general(left, right, (dims, ((), ())), preferred_element_type=jnp...]
    ppermute x0 -> x2, waiting for transfers between devices: none -> 98.4 us  [the longest x1 51.5 us: shards(): half_arrived = lax.ppermute(half_other, 'fsdp', swap).astype(jnp.float32)]
    all_to_all x1, waiting for transfers between devices: 42 us -> 0.01 us  [shards(): lax.all_to_all(outgoing, 'dp', split_axis=1, concat_axis=0, tiled=True)]
    psum x1, blocking collectives: 5.64 us -> 37.4 us  [shards(): grad_step = scale_factor * lax.psum(partial_step, 'dp')]
    all_to_all x2, waiting for transfers between devices: 36.2 us -> 6.27 us  [the longest x1 6.27 us: shards(): lax.all_to_all(out_grads.reshape(own_rows, line_count, 2 * columns), 'fsd...]
    reduce_sum x1 -> x0, other arithmetic: 21.8 us -> none  [shards(): jnp.sum(grad_qweight * (quantized - ratio * slope), axis=0, keepdims=True)]
  transfers between devices with their start and end apart: 6 -> 8, of which waited for: 4 -> 5; matrix products, arithmetic and copies ran while one was open for 20% -> 3% of each run, Pallas kernels for 0% -> 0%
where the time goes in v1:
time: 535 us; the launch traced here: 533 us
  waiting for transfers between devices  328 us (61%)
  blocking collectives  82.6 us (15%)
  matrix products  51.5 us (10%)
  local copies, waits for them, and re-layouts  33.7 us (6%)
  starting transfers between devices  17.6 us (3%)
  between operations  13.8 us (3%)
  other arithmetic  5.61 us (1%)
    all_gather x1, waiting for transfers between devices, shards(): lax.all_gather(act, 'fsdp', axis=0, tiled=True, axis_index_groups=lines)  112 us
    reduce_scatter x1, waiting for transfers between devices, shards(): lax.psum_scatter(partial_hidden.astype(jnp.bfloat16), 'fsdp', scatter_dim...  111 us
    dot_general x6, matrix products, contract(): lax.dot_general(left, right, (dims, ((), ())), preferred_element_type=jnp...  51.5 us
    ppermute x1, waiting for transfers between devices, shards(): half_arrived = lax.ppermute(half_other, 'fsdp', swap).astype(jnp.float32)  51.5 us
    ppermute x1, waiting for transfers between devices, shards(): weight_other = lax.ppermute(weight_own, 'fsdp', swap)  46.9 us
    all_gather x1, blocking collectives, shards(): slots = lax.all_gather(patch_slot, 'dp', axis=0, tiled=True)  45.3 us
    psum x1, blocking collectives, shards(): grad_step = scale_factor * lax.psum(partial_step, 'dp')  37.4 us
    unnamed x15, local copies, waits for them, and re-layouts  23.2 us
  transfers between devices with their start and end apart: 8, of which 5 were waited for; matrix products, arithmetic and copies ran while one was open for 3% of the time, Pallas kernels for 0%

profile of v1, /device:TPU:1, one launch (start us, length us, event | category | flops | bytes accessed | tf_op | source)
XLA Modules:
  0.0 532.8 jit_solution(4664338006152422796)
XLA Ops:
  8.9 5.4 %all-to-all-start = ((bf16[64,4,768]{2,0,1:T(8,128)(2,1)}), bf16[64,4,768]{2,0,1:T(8,128)(2,1)S(1)}, u32[]{:S(2)}, u32[]{:S(2)}) async-start(bf16[64,4,768]{2,0,1:T(8,128)(2,1)} %bitcast.30), calls=%async_computation | async-start | bytes 786432 | tf_op jit(solution)/shard_map/all_to_all | solution.py:48
  14.4 4.6 copy.28
  19.0 6.3 %all-to-all-done = bf16[64,4,768]{2,0,1:T(8,128)(2,1)S(1)} async-done(((bf16[64,4,768]{2,0,1:T(8,128)(2,1)}), bf16[64,4,768]{2,0,1:T(8,128)(2,1)S(1)}, u32[]{:S(2)}, u32[]{:S(2)}) %all-to-all-start) | async-done | bytes 393248 | tf_op jit(solution)/shard_map/all_to_all | solution.py:48
  26.0 5.4 %all-to-all-start.1 = ((bf16[128,4,3072]{0,2,1:T(8,128)(2,1)}), bf16[128,4,3072]{0,2,1:T(8,128)(2,1)S(1)}, u32[]{:S(2)}, u32[]{:S(2)}) async-start(bf16[128,4,3072]{0,2,1:T(8,128)(2,1)} %bitcast.8), calls=%async_computation.2 | async-start | bytes 6291456 | tf_op jit(solution)/shard_map/all_to_all | solution.py:59
  32.2 45.3 %all-gather = s32[4,1,128]{2,1,0:T(1,128)S(1)} all-gather(s32[1,1,128]{2,1,0:T(1,128)S(1)} %bitcast.44), channel_id=1, replica_groups=mesh['fsdp'=8,'dp'=4] {'dp'}, dimensions={0}, use_global_device_ids=true | all-gather | bytes 2560 | tf_op jit(solution)/shard_map/all_gather | solution.py:61
  79.1 3.2 copy.29
  82.3 2.8 multiply_convert_fusion.1
  86.8 111.8 %all-gather.6.cloned.1.call-done = bf16[1024,3072]{1,0:T(8,128)(2,1)} async-done(((bf16[256,3072]{1,0:T(8,128)(2,1)}), bf16[1024,3072]{1,0:T(8,128)(2,1)}) %all-gather.6.cloned.1.call-update) | async-done | bytes 6291472 | tf_op jit(solution)/shard_map/all_gather | solution.py:81
  198.6 7.7 %convolution_convert_fusion.1 = bf16[3072,384]{1,0:T(8,128)(2,1)} fusion(bf16[1024,3072]{1,0:T(8,128)(2,1)} %all-gather.6.cloned.1.call-done, bf16[1024,768]{1,0:T(8,128)(2,1)S(1)} %bitcast.35, s32[]{:T(128)S(6)} %select_n.7), kind=kOutput, calls=%fused_computation.10 | convolution fusion | flops 2417098752 | bytes 9437188 | tf_op jit(solution)/shard_map/dot_general | solution.py:32
  207.5 51.5 %collective-permute-done.1 = bf16[3072,384]{1,0:T(8,128)(2,1)} collective-permute-done((bf16[3072,384]{1,0:T(8,128)(2,1)}, bf16[3072,384]{1,0:T(8,128)(2,1)}, u32[]{:S(2)}, u32[]{:S(2)}) %collective-permute-start.1) | collective-permute-done | bytes 2359328 | tf_op jit(solution)/shard_map/ppermute | solution.py:91
  259.0 25.5 %multiply_reduce_fusion = (f32[384]{0:T(512)S(1)}, f32[3072,384]{1,0:T(8,128)}, bf16[3072,384]{1,0:T(8,128)(2,1)S(1)}) fusion(bf16[3072,384]{1,0:T(8,128)(2,1)} %collective-permute-done.1, f32[384]{0:T(512)S(1)} %convert_reduce_fusion, bf16[3072,384]{1,0:T(8,128)(2,1)} %param.8, bf16[1024,3072]{1,0:T(8,128)(2,1)} %all-gather.6.cloned.1.call-done, ...), kind=kOutput, calls=%fused_computation.2 | convolution fusion | flops 2440691200 | bytes 18877956 | tf_op jit(solution)/shard_map/dot_general | solution.py:32
  285.7 3.5 fusion.15
  289.2 46.9 %collective-permute-done = bf16[3072,384]{1,0:T(8,128)(2,1)} collective-permute-done((bf16[3072,384]{1,0:T(8,128)(2,1)S(1)}, bf16[3072,384]{1,0:T(8,128)(2,1)}, u32[]{:S(2)}, u32[]{:S(2)}) %collective-permute-start) | collective-permute-done | bytes 2359328 | tf_op jit(solution)/shard_map/ppermute | solution.py:68
  336.1 7.1 %add_convert_fusion = bf16[1024,3072]{1,0:T(8,128)(2,1)} fusion(f32[1024,3072]{1,0:T(8,128)S(1)} %fusion.15, bf16[3072,384]{1,0:T(8,128)(2,1)} %collective-permute-done, bf16[1024,768]{1,0:T(8,128)(2,1)S(1)} %bitcast.38, s32[]{:T(128)S(6)} %select_n.7), kind=kOutput, calls=%fused_computation | convolution fusion | flops 2422210560 | bytes 22020100 | tf_op jit(solution)/shard_map/dot_general | solution.py:32
  343.2 110.7 %reduce-scatter.2.cloned.1.call-done = bf16[256,3072]{1,0:T(8,128)(2,1)} async-done(((bf16[1024,3072]{1,0:T(8,128)(2,1)}), bf16[256,3072]{1,0:T(8,128)(2,1)}) %reduce-scatter.2.cloned.1.call-update) | async-done | bytes 1572880 | tf_op jit(solution)/shard_map/reduce_scatter | solution.py:77
  453.9 5.0 fusion.1
  459.4 5.0 reduce.2
  464.4 3.5 reshape.42
  467.9 4.3 all-to-all-start.2
  472.2 37.4 %psum.7 = f32[1,384]{1,0:T(1,128)S(1)} all-reduce(f32[1,384]{1,0:T(1,128)S(1)} %broadcast_in_dim.4), channel_id=1, replica_groups=mesh['fsdp'=8,'dp'=4] {'dp'}, use_global_device_ids=true, to_apply=%region_2.0 | all-reduce | flops 384 | bytes 3072 | tf_op jit(solution)/shard_map/psum | solution.py:96
  510.2 4.3 reshape.43
  514.5 5.6 %copy.33 = bf16[512,1,3072]{2,0,1:T(8,128)(2,1)} copy(bf16[512,1,3072]{2,1,0:T(2,128)(2,1)} %reshape.43) | data formatting | bytes 6291456
  520.0 3.5 copy.31
  523.5 2.8 copy.32
  (27 shorter events, 10.0 us)
Async XLA Ops:
  8.9 16.3 %all-to-all-start = ((bf16[64,4,768]{2,0,1:T(8,128)(2,1)}), bf16[64,4,768]{2,0,1:T(8,128)(2,1)S(1)}, u32[]{:S(2)}, u32[]{:S(2)}) async-start(bf16[64,4,768]{2,0,1:T(8,128)(2,1)} %bitcast.30), calls=%async_computation | async-start | bytes 786432 | tf_op jit(solution)/shard_map/all_to_all | solution.py:48
  25.2 0.8 copy-start.2
  25.2 6.9 %copy-start.4 = (s32[128]{0:T(128)S(1)}, s32[128]{0:T(128)}, u32[]{:S(2)}) copy-start(s32[128]{0:T(128)} %param.6) | copy-start | bytes 1540
  26.0 51.5 %all-to-all-start.1 = ((bf16[128,4,3072]{0,2,1:T(8,128)(2,1)}), bf16[128,4,3072]{0,2,1:T(8,128)(2,1)S(1)}, u32[]{:S(2)}, u32[]{:S(2)}) async-start(bf16[128,4,3072]{0,2,1:T(8,128)(2,1)} %bitcast.8), calls=%async_computation.2 | async-start | bytes 6291456 | tf_op jit(solution)/shard_map/all_to_all | solution.py:59
  31.4 53.8 %all-gather.4.cloned.1.call-start = ((), (), s32[]{:S(2)}) async-start(), calls=%async_computation.4 | async-start | bytes 1966080 | tf_op jit(solution)/shard_map/all_gather | solution.py:52
  32.1 166.5 %all-gather.6.cloned.1.call-start = ((), (), s32[]{:S(2)}) async-start(), calls=%async_computation.6 | async-start | bytes 7864320 | tf_op jit(solution)/shard_map/all_gather | solution.py:81
  77.5 1.7 copy-start
  85.2 368.7 %reduce-scatter.2.cloned.1.call-start = ((), (), s32[]{:S(2)}) async-start(), calls=%async_computation.5 | async-start | bytes 7864320 | tf_op jit(solution)/shard_map/reduce_scatter | solution.py:77
  198.6 8.9 %copy-start.3 = (bf16[1,384]{1,0:T(2,128)(2,1)S(1)}, bf16[1,384]{1,0:T(2,128)(2,1)}, u32[]{:S(2)}) copy-start(bf16[1,384]{1,0:T(2,128)(2,1)} %param.9) | copy-start | bytes 2308
  206.3 52.7 %collective-permute-start.1 = (bf16[3072,384]{1,0:T(8,128)(2,1)}, bf16[3072,384]{1,0:T(8,128)(2,1)}, u32[]{:S(2)}, u32[]{:S(2)}) collective-permute-start(bf16[3072,384]{1,0:T(8,128)(2,1)} %convolution_convert_fusion.1), channel_id=1, source_target_pairs={{0,4},{4,0},{8,12},{12,8},{16,20},{20,16},{24,28},{28,24},{1,5},{5... | collective-permute-start | bytes 7077896 | tf_op jit(solution)/shard_map/ppermute | solution.py:91
  284.5 51.6 %collective-permute-start = (bf16[3072,384]{1,0:T(8,128)(2,1)S(1)}, bf16[3072,384]{1,0:T(8,128)(2,1)}, u32[]{:S(2)}, u32[]{:S(2)}) collective-permute-start(bf16[3072,384]{1,0:T(8,128)(2,1)S(1)} %get-tuple-element.8), channel_id=1, source_target_pairs={{0,4},{4,0},{8,12},{12,8},{16,20},{20,16},{24,28},{28,24},{1,5},{5... | collective-permute-start | bytes 7077896 | tf_op jit(solution)/shard_map/ppermute | solution.py:68
  343.1 110.8 %copy-start.1 = (f32[256,3072]{1,0:T(8,128)S(1)}, f32[256,3072]{1,0:T(8,128)}, u32[]{:S(2)}) copy-start(f32[256,3072]{1,0:T(8,128)} %get-tuple-element.10) | copy-start | bytes 9437188
  467.9 42.2 %all-to-all-start.2 = ((bf16[4,2,196608]{2,1,0:T(2,128)(2,1)}), bf16[4,2,196608]{2,1,0:T(2,128)(2,1)S(1)}, u32[]{:S(2)}, u32[]{:S(2)}) async-start(bf16[4,2,196608]{2,1,0:T(2,128)(2,1)} %reshape.42), calls=%async_computation.3 | async-start | bytes 6291456 | tf_op jit(solution)/shard_map/all_to_all | solution.py:85
Sparse Core Ops, SparseCore 0:
  33.8 27.5 all-gather.3
  85.3 113.2 all-gather.5
  343.3 110.5 reduce-scatter.1

commit v2 on v0

v2 whole, which is shorter than its diff:
```python
import functools

import jax
import jax.numpy as jnp
from jax import lax
from jax.experimental import pallas as pl
from jax.experimental.pallas import tpu as pltpu
from jax.sharding import PartitionSpec as P

FF_W = 12288
CHUNKS = 6
LAG = 1
MESH = pl.DeviceIdType.MESH

top_level = 7.0
wobble = 0.9
two_pi = 6.283185307179586
pi = 3.141592653589793
inv_root_two = 0.7071067811865476
inv_root_tau = 0.3989422804014327


def gelu_pair(values):
    normal_cdf = 0.5 * (1.0 + lax.erf(values * inv_root_two))
    density = jnp.exp(-0.5 * values * values) * inv_root_tau
    return (values * normal_cdf, normal_cdf + values * density)


def sin_cos_turns(turns):
    angle = pi * (turns - jnp.floor(turns + 0.5))
    square = angle * angle
    s = -1.0 / 39916800.0
    for c in (1.0 / 362880.0, -1.0 / 5040.0, 1.0 / 120.0, -1.0 / 6.0, 1.0):
        s = s * square + c
    s = s * angle
    c = 1.0 / 479001600.0
    for k in (-1.0 / 3628800.0, 1.0 / 40320.0, -1.0 / 720.0, 1.0 / 24.0, -0.5, 1.0):
        c = c * square + k
    return 2.0 * s * c, 1.0 - 2.0 * s * s


def soft_quantize(weight, step, inv_step):
    ratio = weight * inv_step
    unit = jnp.tanh(ratio * (1.0 / top_level))
    clipped = top_level * unit
    sine, cosine = sin_cos_turns(clipped)
    quantized = clipped - (wobble / two_pi) * sine
    slope = (1.0 - wobble * cosine) * (1.0 - unit * unit)
    return (step * quantized, slope, quantized - ratio * slope)


def dot(left, right, left_dim, right_dim):
    return lax.dot_general(
        left, right, (((left_dim,), (right_dim,)), ((), ())), preferred_element_type=jnp.float32
    )


def kernel(
    line, dps, acts_hbm, slots_ref, og_ref, latent_ref, step_ref,
    ga_hbm, gw_hbm, gstep_ref,
    inc, slot_all, place, acts, gelu_slope, gz, qw, rr, sl, res, gs, gr, tmp, stp,
    slot_recv, slot_send, ogz_recv, ogz_send, ogd_recv, ogd_send, inc_recv, inc_send,
    qw_recv, qw_send, ag_recv, ag_send, rs_recv, rs_send, gr_recv, gr_send,
    ga_recv, ga_send, gw_sem, st_recv, st_send,
):
    K = inc.shape[0]
    cap, width = inc.shape[2], inc.shape[3]
    rows = acts.shape[2]
    own_rows, cols = og_ref.shape[2], og_ref.shape[3]
    hidden = K * width
    f = lax.axis_index("fsdp")
    d = lax.axis_index("dp")
    me = lax.div(f, 2)
    side = lax.rem(f, 2)
    other = 1 - side

    def at(z, s, e):
        return (z * 2 + s, e)

    partner = at(me, other, d)
    right = at(jnp.minimum(me + 1, line - 1), side, d)
    left = at(jnp.maximum(me - 1, 0), side, d)
    mates = [lax.rem(d + j, dps) for j in range(1, dps)]
    others = [lax.rem(me + j, line) for j in range(1, line)]

    def remote(src, dst, send, recv, device):
        return pltpu.make_async_remote_copy(
            src_ref=src, dst_ref=dst, send_sem=send, recv_sem=recv,
            device_id=device, device_id_type=MESH,
        )

    def await_bytes(ref, sem):
        pltpu.make_async_copy(ref, ref, sem).wait()

    barrier = pltpu.get_barrier_semaphore()
    for z in others:
        pl.semaphore_signal(barrier, inc=1, device_id=at(z, side, d), device_id_type=MESH)
    for e in mates:
        pl.semaphore_signal(barrier, inc=1, device_id=at(me, side, e), device_id_type=MESH)
    pl.semaphore_signal(barrier, inc=1, device_id=partner, device_id_type=MESH)
    pl.semaphore_wait(barrier, line + dps - 1)

    for z in others:
        remote(og_ref.at[z], gz.at[:, me, d], ogz_send, ogz_recv.at[me], at(z, side, d)).start()
    for e in mates:
        remote(slots_ref, slot_all.at[d], slot_send, slot_recv, at(me, side, e)).start()
    slot_all[d] = slots_ref[...]
    gz[:, me, d] = og_ref[me]

    def send_acts(k):
        for e in mates:
            src = acts_hbm.at[:, pl.ds(pl.multiple_of(e * hidden + k * width, 128), width)]
            remote(src, inc.at[k, d], inc_send, inc_recv.at[k], at(me, side, e)).start()
        src = acts_hbm.at[:, pl.ds(pl.multiple_of(d * hidden + k * width, 128), width)]
        pltpu.make_async_copy(src, inc.at[k, d], inc_recv.at[k]).start()

    def forward_grads(z):
        for e in mates:
            remote(gz.at[:, z, d], gz.at[:, z, d], ogd_send, ogd_recv.at[z], at(me, side, e)).start()

    step = step_ref[...].astype(jnp.float32)
    inv_step = 1.0 / step

    def quantize(k):
        block = 16

        def body(i, carry):
            part = pl.ds(pl.multiple_of(i * block, block), block)
            weight = latent_ref[k, part, :].astype(jnp.float32)
            q, slope, rest = soft_quantize(weight, step, inv_step)
            qw[side, k, part, :] = q.astype(jnp.bfloat16)
            sl[k, part, :] = slope
            res[k, part, :] = rest
            return carry

        lax.fori_loop(0, width // block, body, 0)
        remote(qw.at[side, k], qw.at[side, k], qw_send, qw_recv.at[k], partner).start()

    send_acts(0)
    forward_grads(me)
    send_acts(1)
    quantize(0)

    @pl.when((me == 0) | (me == line - 1))
    def _():
        def body(k, carry):
            @pl.when(me == 0)
            def _():
                for z in range(line):
                    rr[k, z] = jnp.zeros((rows, width), jnp.bfloat16)

            @pl.when(me == line - 1)
            def _():
                for z in range(line - 1):
                    rr[k, z] = jnp.zeros((rows, width), jnp.bfloat16)
                rr[k, line] = jnp.zeros((rows, width), jnp.bfloat16)

            return carry

        lax.fori_loop(0, K, body, 0)

    for z in others:
        await_bytes(gz.at[:, z, d], ogz_recv.at[z])
        forward_grads(z)
    quantize(1)
    await_bytes(slot_all.at[pl.ds(0, dps - 1)], slot_recv)
    for e in range(dps):
        place[:, e * cap:(e + 1) * cap] = (
            lax.broadcasted_iota(jnp.int32, (rows, cap), 0) == slot_all[e]
        ).astype(jnp.float32).astype(jnp.bfloat16)
    stp[d] = jnp.zeros((1, cols), jnp.float32)

    def grads_of(s, z):
        return gz[s, z].reshape(rows, cols)

    def partial_hidden(z, k):
        return dot(grads_of(0, z), qw[0, k], 1, 1) + dot(grads_of(1, z), qw[1, k], 1, 1)

    def pack(k):
        await_bytes(inc.at[k], inc_recv.at[k])
        tmp[...] = dot(place[...], inc[k].reshape(dps * cap, width), 1, 0)
        block = 16

        def body(i, carry):
            part = pl.ds(pl.multiple_of(i * block, block), block)
            act, slope = gelu_pair(tmp[part, :])
            acts[k, me, part, :] = act.astype(jnp.bfloat16)
            gelu_slope[k, part, :] = slope
            return carry

        lax.fori_loop(0, rows // block, body, 0)
        send_line(k, me, True, True)

    def send_line(k, z, to_right, to_left):
        block = acts.at[k, z]
        if to_right:
            @pl.when(me < line - 1)
            def _():
                remote(block, block, ag_send, ag_recv.at[k, z], right).start()
        if to_left:
            @pl.when(me > 0)
            def _():
                remote(block, block, ag_send, ag_recv.at[k, z], left).start()

    def hop(k, h):
        @pl.when(me - h >= 0)
        def _():
            z = me - h
            await_bytes(acts.at[k, z], ag_recv.at[k, z])
            send_line(k, z, True, False)

        @pl.when(me + h <= line - 1)
        def _():
            z = me + h
            await_bytes(acts.at[k, z], ag_recv.at[k, z])
            send_line(k, z, False, True)

    def sum_right(k):
        for j in range(line - 1, 0, -1):
            @pl.when(me + j <= line - 1)
            def _():
                z = me + j

                @pl.when(me > 0)
                def _():
                    await_bytes(rr.at[k, z], rs_recv.at[k, z])

                total = rr[k, z].astype(jnp.float32) + partial_hidden(z, k)
                rr[k, z] = total.astype(jnp.bfloat16)
                remote(rr.at[k, z], rr.at[k, z], rs_send, rs_recv.at[k, z], right).start()

    def sum_left(k):
        for j in range(line - 1, 0, -1):
            @pl.when(me - j >= 0)
            def _():
                z = me - j
                slot = line if j == 1 else z

                @pl.when(me < line - 1)
                def _():
                    await_bytes(rr.at[k, z], rs_recv.at[k, z])

                total = rr[k, z].astype(jnp.float32) + partial_hidden(z, k)
                rr[k, z] = total.astype(jnp.bfloat16)
                remote(rr.at[k, z], rr.at[k, slot], rs_send, rs_recv.at[k, slot], left).start()

    def finish_hidden(k):
        @pl.when(me > 0)
        def _():
            await_bytes(rr.at[k, me], rs_recv.at[k, me])

        @pl.when(me < line - 1)
        def _():
            await_bytes(rr.at[k, line], rs_recv.at[k, line])

        total = rr[k, me].astype(jnp.float32) + rr[k, line].astype(jnp.float32) + partial_hidden(me, k)
        packed = (total * gelu_slope[k]).astype(jnp.bfloat16)
        picked = dot(place[...], packed, 0, 0).astype(jnp.bfloat16)
        inc[k] = picked.reshape(dps, cap, width)
        here = ga_hbm.at[:, pl.ds(pl.multiple_of(d * hidden + k * width, 128), width)]
        for e in mates:
            remote(inc.at[k, e], here, ga_send, ga_recv, at(me, side, e)).start()
        pltpu.make_async_copy(inc.at[k, d], here, ga_recv).start()

    def weight_half(k, s):
        return dot(acts[k].reshape(line * rows, width), gz[s].reshape(line * rows, cols), 0, 0)

    def send_half(k):
        gs[k] = weight_half(k, other).astype(jnp.bfloat16)
        remote(gs.at[k], gr.at[k], gr_send, gr_recv.at[k], partner).start()

    def finish_weight(k):
        own = weight_half(k, side)
        await_bytes(gr.at[k], gr_recv.at[k])
        total = own + gr[k].astype(jnp.float32)
        stp[d] += jnp.sum(total * res[k], axis=0, keepdims=True)
        sl[k] = total * sl[k]
        pltpu.make_async_copy(
            sl.at[k], gw_hbm.at[pl.ds(pl.multiple_of(k * width, 16), width), :], gw_sem
        ).start()

    def when_chunk(k, act):
        @pl.when((k >= 0) & (k < K))
        def _():
            act(k)

    def await_grads():
        for z in range(line):
            await_bytes(gz.at[:, z, pl.ds(0, dps - 1)], ogd_recv.at[z])

    depth = LAG * (line - 1)

    def turn(t, carry):
        when_chunk(t, pack)

        @pl.when(t == 0)
        def _():
            await_grads()

        when_chunk(t, lambda k: await_bytes(qw.at[other, k], qw_recv.at[k]))
        for h in range(1, line):
            when_chunk(t - LAG * h, lambda k, h=h: hop(k, h))
        when_chunk(t - LAG * me, sum_right)
        when_chunk(t - LAG * (line - 1 - me), sum_left)

        @pl.when(t + 2 < K)
        def _():
            send_acts(t + 2)
            quantize(t + 2)

        when_chunk(t - depth, finish_hidden)
        when_chunk(t - depth, send_half)
        when_chunk(t - depth - LAG, finish_weight)
        return carry

    lax.fori_loop(0, K + depth + LAG, turn, 0)

    for e in mates:
        remote(stp.at[d], stp.at[d], st_send, st_recv, at(me, side, e)).start()
    await_bytes(stp.at[pl.ds(0, dps - 1)], st_recv)
    total = stp[0]
    for e in range(1, dps):
        total = total + stp[e]
    gstep_ref[...] = ((FF_W * top_level) ** (-0.5)) * total

    await_bytes(stp.at[pl.ds(0, dps - 1)], st_send)
    await_bytes(slot_all.at[pl.ds(0, dps - 1)], slot_send)
    await_bytes(gz.at[:, pl.ds(0, line - 1), 0], ogz_send)
    await_bytes(gz.at[:, :, pl.ds(0, dps - 1)], ogd_send)
    await_bytes(inc.at[:, pl.ds(0, dps - 1)], inc_send)
    await_bytes(qw.at[0], qw_send)
    await_bytes(gs, gr_send)
    await_bytes(rr.at[:, pl.ds(0, line - 1)], rs_send)

    @pl.when((me == 0) | (me == line - 1))
    def _():
        await_bytes(acts.at[:, 0], ag_send)

    @pl.when((me > 0) & (me < line - 1))
    def _():
        await_bytes(rr, ag_send)

    await_bytes(inc.at[:, pl.ds(0, dps - 1)], ga_send)
    await_bytes(inc, ga_recv)
    await_bytes(sl, gw_sem)


def shards(patch_acts, patch_slot, out_grads, latent_weight, step_size):
    dps = lax.axis_size("dp")
    line = lax.axis_size("fsdp") // 2
    cap, features = patch_acts.shape
    hidden = features // dps
    own_rows, all_columns = out_grads.shape
    rows = own_rows * dps
    cols = latent_weight.shape[1]
    K = CHUNKS
    width = hidden // K
    grads = out_grads.reshape(own_rows, line, 2, cols).transpose(1, 2, 0, 3)
    bf16, f32 = jnp.bfloat16, jnp.float32
    vmem = pl.BlockSpec(memory_space=pltpu.VMEM)
    hbm = pl.BlockSpec(memory_space=pl.ANY)
    dma = pltpu.SemaphoreType.DMA
    return pl.pallas_call(
        functools.partial(kernel, line, dps),
        out_shape=(
            jax.ShapeDtypeStruct((cap, features), bf16),
            jax.ShapeDtypeStruct((hidden, cols), f32),
            jax.ShapeDtypeStruct((1, cols), f32),
        ),
        in_specs=[hbm, vmem, vmem, vmem, vmem],
        out_specs=(hbm, hbm, vmem),
        scratch_shapes=[
            pltpu.VMEM((K, dps, cap, width), bf16),
            pltpu.VMEM((dps, 1, cap), jnp.int32),
            pltpu.VMEM((rows, dps * cap), bf16),
            pltpu.VMEM((K, line, rows, width), bf16),
            pltpu.VMEM((K, rows, width), f32),
            pltpu.VMEM((2, line, dps, own_rows, cols), bf16),
            pltpu.VMEM((2, K, width, cols), bf16),
            pltpu.VMEM((K, line + 1, rows, width), bf16),
            pltpu.VMEM((K, width, cols), f32),
            pltpu.VMEM((K, width, cols), f32),
            pltpu.VMEM((K, width, cols), bf16),
            pltpu.VMEM((K, width, cols), bf16),
            pltpu.VMEM((rows, width), f32),
            pltpu.VMEM((dps, 1, cols), f32),
            dma, dma, dma((line,)), dma, dma((line,)), dma, dma((K,)), dma,
            dma((K,)), dma, dma((K, line)), dma, dma((K, line + 1)), dma, dma((K,)), dma,
            dma, dma, dma, dma, dma,
        ],
        compiler_params=pltpu.CompilerParams(
            collective_id=0, has_side_effects=True, vmem_limit_bytes=60 * 1024 * 1024
        ),
        cost_estimate=pl.CostEstimate(
            flops=8 * line * rows * hidden * cols, bytes_accessed=4 * cap * features,
            transcendentals=0,
        ),
    )(patch_acts, patch_slot.reshape(1, cap), grads, latent_weight.reshape(K, width, cols), step_size)


def solution(mesh):
    return jax.shard_map(
        shards,
        mesh=mesh,
        in_specs=(
            P(("fsdp", "dp"), None),
            P(("fsdp", "dp")),
            P(("fsdp", "dp"), None),
            P("dp", "fsdp"),
            P(None, "fsdp"),
        ),
        out_specs=(P(("fsdp", "dp"), None), P("dp", "fsdp"), P(None, "fsdp")),
        check_vma=False,
    )
```

time: 1050 us -> 209 us (0.20)
  waiting for transfers between devices: 757 us -> 0 us
  Pallas kernels: 0 us -> 199 us
  matrix products: 161 us -> 0 us
  local copies, waits for them, and re-layouts: 39.8 us -> 8.81 us
  blocking collectives: 30.9 us -> 0 us
  other arithmetic: 28.5 us -> 0 us
  between operations: 13.8 us -> 0.65 us
  starting transfers between devices: 12.4 us -> 0 us
    reduce_scatter x1 -> x0, waiting for transfers between devices: 391 us -> none  [shards(): lax.psum_scatter(contract_first(columns, act), 'fsdp', scatter_dimension=...]
    all_gather x2 -> x0, waiting for transfers between devices: 286 us -> none  [the longest x1 286 us: shards(): lax.all_gather(latent_weight, 'fsdp', axis=1, tiled=True)]
    pallas_call x0 -> x1, Pallas kernels: none -> 199 us  [shards(): pl.pallas_call(functools.partial(kernel, line, dps), out_shape=(jax.Shape...]
    dot_general x2 -> x0, matrix products: 161 us -> none  [the longest x1 144 us: contract_last(): lax.dot_general(left, right, (((1,), (1,)), ((), ())), preferred_element_...]
    all_to_all x3 -> x0, waiting for transfers between devices: 78.2 us -> none  [the longest x1 42 us: shards(): lax.all_to_all(outgoing, 'dp', split_axis=1, concat_axis=0, tiled=True)]
    all_gather x1 -> x0, blocking collectives: 25.3 us -> none  [shards(): lax.all_gather(step_size, 'fsdp', axis=1, tiled=True).astype(jnp.float32)]
    reduce_sum x1 -> x0, other arithmetic: 21.8 us -> none  [shards(): jnp.sum(grad_qweight * (quantized - ratio * slope), axis=0, keepdims=True)]
    unnamed x10 -> x7, local copies, waits for them, and re-layouts: 20.2 us -> 6.74 us
  transfers between devices with their start and end apart: 6 -> 0, of which waited for: 4 -> 0; matrix products, arithmetic and copies ran while one was open for 20% -> 0% of each run, Pallas kernels for 0% -> 0%
where the time goes in v2:
time: 209 us; the launch traced here: 208 us
  Pallas kernels  199 us (95%)
  local copies, waits for them, and re-layouts  8.81 us (4%)
    pallas_call x1, Pallas kernels, shards(): pl.pallas_call(functools.partial(kernel, line, dps), out_shape=(jax.Shape...  199 us
    unnamed x7, local copies, waits for them, and re-layouts  6.74 us

profile of v2, /device:TPU:1, one launch (start us, length us, event | category | flops | bytes accessed | tf_op | source)
XLA Modules:
  0.0 208.2 jit_solution(3122555909578263139)
XLA Ops:
  0.6 1.3 reshape.16
  1.9 0.8 copy.10
  2.7 198.7 %shard_map.76 = (bf16[128,12288]{1,0:T(8,128)(2,1)}, f32[3072,384]{1,0:T(8,128)}, f32[1,384]{1,0:T(1,128)}) custom-call(bf16[128,12288]{1,0:T(8,128)(2,1)} %acts_hbm.1, s32[1,128]{1,0:T(1,128)} %bitcast.7, bf16[4,2,64,384]{3,2,1,0:T(8,128)(2,1)} %bitcast.5, bf16[6,512,384]{2,1,0:T(8,128)(2,1)} %bitcast.6, bf16[1,384]{1,0:T(2,128)(2,1)} %step_ref.1), custom_call_target="tpu_custom_call" | custom-call | flops 9663676416 | bytes 6291456 | tf_op jit(solution)/shard_map/pallas_call | solution.py:363
  201.4 0.0 copy-start
  201.5 4.0 %copy.14 = bf16[128,12288]{1,0:T(8,128)(2,1)} copy(bf16[128,12288]{1,0:T(8,128)(2,1)} %get-tuple-element.6) | data formatting | bytes 6291456
  205.4 0.0 copy-done
  205.4 0.0 copy-start.1
  205.4 2.2 %copy.15 = f32[3072,384]{1,0:T(8,128)} copy(f32[3072,384]{1,0:T(8,128)S(1)} %copy-done) | data formatting | bytes 9437184
  207.6 0.0 copy-done.1
  207.6 0.6 copy.16
Async XLA Ops:
  201.4 4.0 %copy-start = (f32[3072,384]{1,0:T(8,128)S(1)}, f32[3072,384]{1,0:T(8,128)}, u32[]{:S(2)}) copy-start(f32[3072,384]{1,0:T(8,128)} %get-tuple-element.7) | copy-start | bytes 14155780
  205.4 2.2 %copy-start.1 = (f32[1,384]{1,0:T(1,128)S(1)}, f32[1,384]{1,0:T(1,128)}, u32[]{:S(2)}) copy-start(f32[1,384]{1,0:T(1,128)} %get-tuple-element.8) | copy-start | bytes 4612

commit v3 on v2

--- a/solution.py
+++ b/solution.py
@@ -8,8 +8,10 @@
 from jax.sharding import PartitionSpec as P
 
 FF_W = 12288
-CHUNKS = 6
-LAG = 1
+CHUNKS = 12
+LAG = 2
+BEHIND = 2
+AHEAD = 4
 MESH = pl.DeviceIdType.MESH
 
 top_level = 7.0
@@ -122,7 +124,7 @@
     inv_step = 1.0 / step
 
     def quantize(k):
-        block = 16
+        block = 32
 
         def body(i, carry):
             part = pl.ds(pl.multiple_of(i * block, block), block)
@@ -136,39 +138,20 @@
         lax.fori_loop(0, width // block, body, 0)
         remote(qw.at[side, k], qw.at[side, k], qw_send, qw_recv.at[k], partner).start()
 
-    send_acts(0)
-    forward_grads(me)
-    send_acts(1)
+    for k in range(min(AHEAD, K)):
+        send_acts(k)
+        if k == 0:
+            forward_grads(me)
+    stp[d] = jnp.zeros((1, cols), jnp.float32)
     quantize(0)
-
-    @pl.when((me == 0) | (me == line - 1))
-    def _():
-        def body(k, carry):
-            @pl.when(me == 0)
-            def _():
-                for z in range(line):
-                    rr[k, z] = jnp.zeros((rows, width), jnp.bfloat16)
-
-            @pl.when(me == line - 1)
-            def _():
-                for z in range(line - 1):
-                    rr[k, z] = jnp.zeros((rows, width), jnp.bfloat16)
-                rr[k, line] = jnp.zeros((rows, width), jnp.bfloat16)
-
-            return carry
-
-        lax.fori_loop(0, K, body, 0)
-
-    for z in others:
-        await_bytes(gz.at[:, z, d], ogz_recv.at[z])
-        forward_grads(z)
-    quantize(1)
     await_bytes(slot_all.at[pl.ds(0, dps - 1)], slot_recv)
     for e in range(dps):
         place[:, e * cap:(e + 1) * cap] = (
             lax.broadcasted_iota(jnp.int32, (rows, cap), 0) == slot_all[e]
         ).astype(jnp.float32).astype(jnp.bfloat16)
-    stp[d] = jnp.zeros((1, cols), jnp.float32)
+
+    def clear(k, slot):
+        rr[k, slot] = jnp.zeros((rows, width), jnp.bfloat16)
 
     def grads_of(s, z):
         return gz[s, z].reshape(rows, cols)
@@ -179,7 +162,7 @@
     def pack(k):
         await_bytes(inc.at[k], inc_recv.at[k])
         tmp[...] = dot(place[...], inc[k].reshape(dps * cap, width), 1, 0)
-        block = 16
+        block = 32
 
         def body(i, carry):
             part = pl.ds(pl.multiple_of(i * block, block), block)
@@ -225,6 +208,10 @@
                 def _():
                     await_bytes(rr.at[k, z], rs_recv.at[k, z])
 
+                @pl.when(me == 0)
+                def _():
+                    clear(k, z)
+
                 total = rr[k, z].astype(jnp.float32) + partial_hidden(z, k)
                 rr[k, z] = total.astype(jnp.bfloat16)
                 remote(rr.at[k, z], rr.at[k, z], rs_send, rs_recv.at[k, z], right).start()
@@ -240,6 +227,10 @@
                 def _():
                     await_bytes(rr.at[k, z], rs_recv.at[k, z])
 
+                @pl.when(me == line - 1)
+                def _():
+                    clear(k, z)
+
                 total = rr[k, z].astype(jnp.float32) + partial_hidden(z, k)
                 rr[k, z] = total.astype(jnp.bfloat16)
                 remote(rr.at[k, z], rr.at[k, slot], rs_send, rs_recv.at[k, slot], left).start()
@@ -252,6 +243,14 @@
         @pl.when(me < line - 1)
         def _():
             await_bytes(rr.at[k, line], rs_recv.at[k, line])
+
+        @pl.when(me == 0)
+        def _():
+            clear(k, me)
+
+        @pl.when(me == line - 1)
+        def _():
+            clear(k, line)
 
         total = rr[k, me].astype(jnp.float32) + rr[k, line].astype(jnp.float32) + partial_hidden(me, k)
         packed = (total * gelu_slope[k]).astype(jnp.bfloat16)
@@ -295,25 +294,35 @@
 
         @pl.when(t == 0)
         def _():
-            await_grads()
-
-        when_chunk(t, lambda k: await_bytes(qw.at[other, k], qw_recv.at[k]))
+            for z in others:
+                await_bytes(gz.at[:, z, d], ogz_recv.at[z])
+                forward_grads(z)
+
         for h in range(1, line):
             when_chunk(t - LAG * h, lambda k, h=h: hop(k, h))
-        when_chunk(t - LAG * me, sum_right)
-        when_chunk(t - LAG * (line - 1 - me), sum_left)
-
-        @pl.when(t + 2 < K)
-        def _():
-            send_acts(t + 2)
-            quantize(t + 2)
-
-        when_chunk(t - depth, finish_hidden)
+
+        @pl.when(t == BEHIND)
+        def _():
+            await_grads()
+
+        when_chunk(t - BEHIND, lambda k: await_bytes(qw.at[other, k], qw_recv.at[k]))
+        when_chunk(t - BEHIND - LAG * me, sum_right)
+        when_chunk(t - BEHIND - LAG * (line - 1 - me), sum_left)
+
+        @pl.when(t + AHEAD < K)
+        def _():
+            send_acts(t + AHEAD)
+
+        @pl.when(t + 1 < K)
+        def _():
+            quantize(t + 1)
+
+        when_chunk(t - BEHIND - depth, finish_hidden)
         when_chunk(t - depth, send_half)
         when_chunk(t - depth - LAG, finish_weight)
         return carry
 
-    lax.fori_loop(0, K + depth + LAG, turn, 0)
+    lax.fori_loop(0, K + depth + max(LAG, BEHIND), turn, 0)
 
     for e in mates:
         remote(stp.at[d], stp.at[d], st_send, st_recv, at(me, side, e)).start()
@@ -353,7 +362,7 @@
     own_rows, all_columns = out_grads.shape
     rows = own_rows * dps
     cols = latent_weight.shape[1]
-    K = CHUNKS
+    K = min(CHUNKS, hidden // 128)
     width = hidden // K
     grads = out_grads.reshape(own_rows, line, 2, cols).transpose(1, 2, 0, 3)
     bf16, f32 = jnp.bfloat16, jnp.float32

time: 209 us -> 191 us (0.914)
  Pallas kernels: 199 us -> 180 us
    pallas_call x1, Pallas kernels: 199 us -> 180 us  [shards(): pl.pallas_call(functools.partial(kernel, line, dps), out_shape=(jax.Shape...]
where the time goes in v3:
time: 191 us; the launch traced here: 189 us
  Pallas kernels  180 us (94%)
  local copies, waits for them, and re-layouts  8.81 us (5%)
    pallas_call x1, Pallas kernels, shards(): pl.pallas_call(functools.partial(kernel, line, dps), out_shape=(jax.Shape...  180 us
    unnamed x7, local copies, waits for them, and re-layouts  6.74 us

profile of v3, /device:TPU:1, one launch (start us, length us, event | category | flops | bytes accessed | tf_op | source)
XLA Modules:
  0.0 189.5 jit_solution(3367970345396274216)
XLA Ops:
  0.6 1.3 reshape.16
  1.9 0.8 copy.10
  2.7 180.0 %shard_map.76 = (bf16[128,12288]{1,0:T(8,128)(2,1)}, f32[3072,384]{1,0:T(8,128)}, f32[1,384]{1,0:T(1,128)}) custom-call(bf16[128,12288]{1,0:T(8,128)(2,1)} %acts_hbm.1, s32[1,128]{1,0:T(1,128)} %bitcast.7, bf16[4,2,64,384]{3,2,1,0:T(8,128)(2,1)} %bitcast.5, bf16[12,256,384]{2,1,0:T(8,128)(2,1)} %bitcast.6, bf16[1,384]{1,0:T(2,128)(2,1)} %step_ref.1), custom_call_target="tpu_custom_call" | custom-call | flops 9663676416 | bytes 6291456 | tf_op jit(solution)/shard_map/pallas_call | solution.py:372
  182.8 0.0 copy-start
  182.8 4.0 %copy.14 = bf16[128,12288]{1,0:T(8,128)(2,1)} copy(bf16[128,12288]{1,0:T(8,128)(2,1)} %get-tuple-element.6) | data formatting | bytes 6291456
  186.7 0.0 copy-done
  186.7 0.0 copy-start.1
  186.7 2.2 %copy.15 = f32[3072,384]{1,0:T(8,128)} copy(f32[3072,384]{1,0:T(8,128)S(1)} %copy-done) | data formatting | bytes 9437184
  188.9 0.0 copy-done.1
  188.9 0.6 copy.16
Async XLA Ops:
  182.8 4.0 %copy-start = (f32[3072,384]{1,0:T(8,128)S(1)}, f32[3072,384]{1,0:T(8,128)}, u32[]{:S(2)}) copy-start(f32[3072,384]{1,0:T(8,128)} %get-tuple-element.7) | copy-start | bytes 14155780
  186.7 2.2 %copy-start.1 = (f32[1,384]{1,0:T(1,128)S(1)}, f32[1,384]{1,0:T(1,128)}, u32[]{:S(2)}) copy-start(f32[1,384]{1,0:T(1,128)} %get-tuple-element.8) | copy-start | bytes 4612

commit v4 on v3

--- a/solution.py
+++ b/solution.py
@@ -10,7 +10,7 @@
 FF_W = 12288
 CHUNKS = 12
 LAG = 2
-BEHIND = 2
+BEHIND = 4
 AHEAD = 4
 MESH = pl.DeviceIdType.MESH
 
@@ -138,10 +138,8 @@
         lax.fori_loop(0, width // block, body, 0)
         remote(qw.at[side, k], qw.at[side, k], qw_send, qw_recv.at[k], partner).start()
 
-    for k in range(min(AHEAD, K)):
-        send_acts(k)
-        if k == 0:
-            forward_grads(me)
+    send_acts(0)
+    forward_grads(me)
     stp[d] = jnp.zeros((1, cols), jnp.float32)
     quantize(0)
     await_bytes(slot_all.at[pl.ds(0, dps - 1)], slot_recv)
@@ -149,6 +147,12 @@
         place[:, e * cap:(e + 1) * cap] = (
             lax.broadcasted_iota(jnp.int32, (rows, cap), 0) == slot_all[e]
         ).astype(jnp.float32).astype(jnp.bfloat16)
+    send_acts(1)
+    for z in others:
+        await_bytes(gz.at[:, z, d], ogz_recv.at[z])
+        forward_grads(z)
+    for k in range(2, min(AHEAD, K)):
+        send_acts(k)
 
     def clear(k, slot):
         rr[k, slot] = jnp.zeros((rows, width), jnp.bfloat16)
@@ -292,12 +296,6 @@
     def turn(t, carry):
         when_chunk(t, pack)
 
-        @pl.when(t == 0)
-        def _():
-            for z in others:
-                await_bytes(gz.at[:, z, d], ogz_recv.at[z])
-                forward_grads(z)
-
         for h in range(1, line):
             when_chunk(t - LAG * h, lambda k, h=h: hop(k, h))
 
@@ -320,12 +318,16 @@
         when_chunk(t - BEHIND - depth, finish_hidden)
         when_chunk(t - depth, send_half)
         when_chunk(t - depth - LAG, finish_weight)
+
+        @pl.when(t == K - 1 + depth + LAG)
+        def _():
+            for e in mates:
+                remote(stp.at[d], stp.at[d], st_send, st_recv, at(me, side, e)).start()
+
         return carry
 
     lax.fori_loop(0, K + depth + max(LAG, BEHIND), turn, 0)
 
-    for e in mates:
-        remote(stp.at[d], stp.at[d], st_send, st_recv, at(me, side, e)).start()
     await_bytes(stp.at[pl.ds(0, dps - 1)], st_recv)
     total = stp[0]
     for e in range(1, dps):

time: 191 us -> 190 us (level)
  no operation moved by 1% of the time
where the time goes in v4:
time: 190 us
  Pallas kernels  181 us (95%)
  local copies, waits for them, and re-layouts  8.81 us (5%)
    pallas_call x1, Pallas kernels, shards(): pl.pallas_call(functools.partial(kernel, line, dps), out_shape=(jax.Shape...  181 us
    unnamed x7, local copies, waits for them, and re-layouts  6.74 us

profile of v4, /device:TPU:1, one launch (start us, length us, event | category | flops | bytes accessed | tf_op | source)
XLA Modules:
  0.0 190.0 jit_solution(7484005772629615603)
XLA Ops:
  0.6 1.3 reshape.16
  1.9 0.8 copy.10
  2.7 180.5 %shard_map.76 = (bf16[128,12288]{1,0:T(8,128)(2,1)}, f32[3072,384]{1,0:T(8,128)}, f32[1,384]{1,0:T(1,128)}) custom-call(bf16[128,12288]{1,0:T(8,128)(2,1)} %acts_hbm.1, s32[1,128]{1,0:T(1,128)} %bitcast.7, bf16[4,2,64,384]{3,2,1,0:T(8,128)(2,1)} %bitcast.5, bf16[12,256,384]{2,1,0:T(8,128)(2,1)} %bitcast.6, bf16[1,384]{1,0:T(2,128)(2,1)} %step_ref.1), custom_call_target="tpu_custom_call" | custom-call | flops 9663676416 | bytes 6291456 | tf_op jit(solution)/shard_map/pallas_call | solution.py:374
  183.3 0.0 copy-start
  183.3 4.0 %copy.14 = bf16[128,12288]{1,0:T(8,128)(2,1)} copy(bf16[128,12288]{1,0:T(8,128)(2,1)} %get-tuple-element.6) | data formatting | bytes 6291456
  187.2 0.0 copy-done
  187.2 0.0 copy-start.1
  187.2 2.2 %copy.15 = f32[3072,384]{1,0:T(8,128)} copy(f32[3072,384]{1,0:T(8,128)S(1)} %copy-done) | data formatting | bytes 9437184
  189.4 0.0 copy-done.1
  189.4 0.6 copy.16
Async XLA Ops:
  183.3 4.0 %copy-start = (f32[3072,384]{1,0:T(8,128)S(1)}, f32[3072,384]{1,0:T(8,128)}, u32[]{:S(2)}) copy-start(f32[3072,384]{1,0:T(8,128)} %get-tuple-element.7) | copy-start | bytes 14155780
  187.2 2.2 %copy-start.1 = (f32[1,384]{1,0:T(1,128)S(1)}, f32[1,384]{1,0:T(1,128)}, u32[]{:S(2)}) copy-start(f32[1,384]{1,0:T(1,128)} %get-tuple-element.8) | copy-start | bytes 4612

commit v5 on v4

--- a/solution.py
+++ b/solution.py
@@ -9,8 +9,8 @@
 
 FF_W = 12288
 CHUNKS = 12
-LAG = 2
-BEHIND = 4
+LAG = 1
+BEHIND = 2
 AHEAD = 4
 MESH = pl.DeviceIdType.MESH
 

time: 190 us -> 188 us (0.989)
  Pallas kernels: 181 us -> 179 us
    pallas_call x1, Pallas kernels: 181 us -> 179 us  [shards(): pl.pallas_call(functools.partial(kernel, line, dps), out_shape=(jax.Shape...]
where the time goes in v5:
time: 188 us
  Pallas kernels  179 us (95%)
  local copies, waits for them, and re-layouts  8.81 us (5%)
    pallas_call x1, Pallas kernels, shards(): pl.pallas_call(functools.partial(kernel, line, dps), out_shape=(jax.Shape...  179 us
    unnamed x7, local copies, waits for them, and re-layouts  6.74 us

profile of v5, /device:TPU:1, one launch (start us, length us, event | category | flops | bytes accessed | tf_op | source)
XLA Modules:
  0.0 188.0 jit_solution(9153662714008185103)
XLA Ops:
  0.6 1.3 reshape.16
  1.9 0.8 copy.10
  2.7 178.5 %shard_map.76 = (bf16[128,12288]{1,0:T(8,128)(2,1)}, f32[3072,384]{1,0:T(8,128)}, f32[1,384]{1,0:T(1,128)}) custom-call(bf16[128,12288]{1,0:T(8,128)(2,1)} %acts_hbm.1, s32[1,128]{1,0:T(1,128)} %bitcast.7, bf16[4,2,64,384]{3,2,1,0:T(8,128)(2,1)} %bitcast.5, bf16[12,256,384]{2,1,0:T(8,128)(2,1)} %bitcast.6, bf16[1,384]{1,0:T(2,128)(2,1)} %step_ref.1), custom_call_target="tpu_custom_call" | custom-call | flops 9663676416 | bytes 6291456 | tf_op jit(solution)/shard_map/pallas_call | solution.py:374
  181.2 0.0 copy-start
  181.2 4.0 %copy.14 = bf16[128,12288]{1,0:T(8,128)(2,1)} copy(bf16[128,12288]{1,0:T(8,128)(2,1)} %get-tuple-element.6) | data formatting | bytes 6291456
  185.2 0.0 copy-done
  185.2 0.0 copy-start.1
  185.2 2.2 %copy.15 = f32[3072,384]{1,0:T(8,128)} copy(f32[3072,384]{1,0:T(8,128)S(1)} %copy-done) | data formatting | bytes 9437184
  187.4 0.0 copy-done.1
  187.4 0.6 copy.16
Async XLA Ops:
  181.2 4.0 %copy-start = (f32[3072,384]{1,0:T(8,128)S(1)}, f32[3072,384]{1,0:T(8,128)}, u32[]{:S(2)}) copy-start(f32[3072,384]{1,0:T(8,128)} %get-tuple-element.7) | copy-start | bytes 14155780
  185.2 2.2 %copy-start.1 = (f32[1,384]{1,0:T(1,128)S(1)}, f32[1,384]{1,0:T(1,128)}, u32[]{:S(2)}) copy-start(f32[1,384]{1,0:T(1,128)} %get-tuple-element.8) | copy-start | bytes 4612

commit v6 on v5

--- a/solution.py
+++ b/solution.py
@@ -60,15 +60,15 @@
 def kernel(
     line, dps, acts_hbm, slots_ref, og_ref, latent_ref, step_ref,
     ga_hbm, gw_hbm, gstep_ref,
-    inc, slot_all, place, acts, gelu_slope, gz, qw, rr, sl, res, gs, gr, tmp, stp,
+    inc, slot_all, place, picks, acts, gelu_slope, gz, qw, rr, sl, res, gs, gr, own, tmp, act, quant, stp,
     slot_recv, slot_send, ogz_recv, ogz_send, ogd_recv, ogd_send, inc_recv, inc_send,
     qw_recv, qw_send, ag_recv, ag_send, rs_recv, rs_send, gr_recv, gr_send,
     ga_recv, ga_send, gw_sem, st_recv, st_send,
 ):
     K = inc.shape[0]
     cap, width = inc.shape[2], inc.shape[3]
-    rows = acts.shape[2]
-    own_rows, cols = og_ref.shape[2], og_ref.shape[3]
+    rows = acts.shape[3]
+    own_rows, cols = og_ref.shape[0], sl.shape[2]
     hidden = K * width
     f = lax.axis_index("fsdp")
     d = lax.axis_index("dp")
@@ -102,12 +102,15 @@
     pl.semaphore_signal(barrier, inc=1, device_id=partner, device_id_type=MESH)
     pl.semaphore_wait(barrier, line + dps - 1)
 
+    def og_of(z):
+        return og_ref.at[:, pl.ds(pl.multiple_of(z * 2 * cols, 128), 2 * cols)]
+
     for z in others:
-        remote(og_ref.at[z], gz.at[:, me, d], ogz_send, ogz_recv.at[me], at(z, side, d)).start()
+        remote(og_of(z), gz.at[me, d], ogz_send, ogz_recv.at[me], at(z, side, d)).start()
     for e in mates:
         remote(slots_ref, slot_all.at[d], slot_send, slot_recv, at(me, side, e)).start()
     slot_all[d] = slots_ref[...]
-    gz[:, me, d] = og_ref[me]
+    gz[me, d] = og_of(me)[...]
 
     def send_acts(k):
         for e in mates:
@@ -118,10 +121,13 @@
 
     def forward_grads(z):
         for e in mates:
-            remote(gz.at[:, z, d], gz.at[:, z, d], ogd_send, ogd_recv.at[z], at(me, side, e)).start()
+            remote(gz.at[z, d], gz.at[z, d], ogd_send, ogd_recv.at[z], at(me, side, e)).start()
 
     step = step_ref[...].astype(jnp.float32)
     inv_step = 1.0 / step
+
+    def qw_of(k, s):
+        return qw.at[k, pl.ds(pl.multiple_of(s * cols, 128), cols)]
 
     def quantize(k):
         block = 32
@@ -130,13 +136,15 @@
             part = pl.ds(pl.multiple_of(i * block, block), block)
             weight = latent_ref[k, part, :].astype(jnp.float32)
             q, slope, rest = soft_quantize(weight, step, inv_step)
-            qw[side, k, part, :] = q.astype(jnp.bfloat16)
+            quant[part, :] = q.astype(jnp.bfloat16)
             sl[k, part, :] = slope
             res[k, part, :] = rest
             return carry
 
         lax.fori_loop(0, width // block, body, 0)
-        remote(qw.at[side, k], qw.at[side, k], qw_send, qw_recv.at[k], partner).start()
+        mine = qw_of(k, side)
+        mine[...] = quant[...].T
+        remote(mine, mine, qw_send, qw_recv.at[k], partner).start()
 
     send_acts(0)
     forward_grads(me)
@@ -144,12 +152,12 @@
     quantize(0)
     await_bytes(slot_all.at[pl.ds(0, dps - 1)], slot_recv)
     for e in range(dps):
-        place[:, e * cap:(e + 1) * cap] = (
-            lax.broadcasted_iota(jnp.int32, (rows, cap), 0) == slot_all[e]
-        ).astype(jnp.float32).astype(jnp.bfloat16)
+        hit = (lax.broadcasted_iota(jnp.int32, (rows, cap), 0) == slot_all[e]).astype(jnp.float32)
+        place[:, e * cap:(e + 1) * cap] = hit.astype(jnp.bfloat16)
+        picks[e * cap:(e + 1) * cap, :] = hit.T.astype(jnp.bfloat16)
     send_acts(1)
     for z in others:
-        await_bytes(gz.at[:, z, d], ogz_recv.at[z])
+        await_bytes(gz.at[z, d], ogz_recv.at[z])
         forward_grads(z)
     for k in range(2, min(AHEAD, K)):
         send_acts(k)
@@ -157,11 +165,8 @@
     def clear(k, slot):
         rr[k, slot] = jnp.zeros((rows, width), jnp.bfloat16)
 
-    def grads_of(s, z):
-        return gz[s, z].reshape(rows, cols)
-
     def partial_hidden(z, k):
-        return dot(grads_of(0, z), qw[0, k], 1, 1) + dot(grads_of(1, z), qw[1, k], 1, 1)
+        return dot(gz[z].reshape(rows, 2 * cols), qw[k], 1, 0)
 
     def pack(k):
         await_bytes(inc.at[k], inc_recv.at[k])
@@ -170,12 +175,13 @@
 
         def body(i, carry):
             part = pl.ds(pl.multiple_of(i * block, block), block)
-            act, slope = gelu_pair(tmp[part, :])
-            acts[k, me, part, :] = act.astype(jnp.bfloat16)
+            value, slope = gelu_pair(tmp[part, :])
+            act[part, :] = value.astype(jnp.bfloat16)
             gelu_slope[k, part, :] = slope
             return carry
 
         lax.fori_loop(0, rows // block, body, 0)
+        acts[k, me] = act[...].T
         send_line(k, me, True, True)
 
     def send_line(k, z, to_right, to_left):
@@ -258,24 +264,24 @@
 
         total = rr[k, me].astype(jnp.float32) + rr[k, line].astype(jnp.float32) + partial_hidden(me, k)
         packed = (total * gelu_slope[k]).astype(jnp.bfloat16)
-        picked = dot(place[...], packed, 0, 0).astype(jnp.bfloat16)
+        picked = dot(picks[...], packed, 1, 0).astype(jnp.bfloat16)
         inc[k] = picked.reshape(dps, cap, width)
         here = ga_hbm.at[:, pl.ds(pl.multiple_of(d * hidden + k * width, 128), width)]
         for e in mates:
             remote(inc.at[k, e], here, ga_send, ga_recv, at(me, side, e)).start()
         pltpu.make_async_copy(inc.at[k, d], here, ga_recv).start()
 
-    def weight_half(k, s):
-        return dot(acts[k].reshape(line * rows, width), gz[s].reshape(line * rows, cols), 0, 0)
-
     def send_half(k):
-        gs[k] = weight_half(k, other).astype(jnp.bfloat16)
+        gathered = jnp.concatenate([acts[k, z] for z in range(line)], axis=1)
+        both = dot(gathered, gz[...].reshape(line * rows, 2 * cols), 1, 0)
+        low, high = both[:, :cols], both[:, cols:]
+        gs[k] = jnp.where(side == 0, high, low).astype(jnp.bfloat16)
         remote(gs.at[k], gr.at[k], gr_send, gr_recv.at[k], partner).start()
+        own[lax.rem(k, LAG + 1)] = jnp.where(side == 0, low, high)
 
     def finish_weight(k):
-        own = weight_half(k, side)
         await_bytes(gr.at[k], gr_recv.at[k])
-        total = own + gr[k].astype(jnp.float32)
+        total = own[lax.rem(k, LAG + 1)] + gr[k].astype(jnp.float32)
         stp[d] += jnp.sum(total * res[k], axis=0, keepdims=True)
         sl[k] = total * sl[k]
         pltpu.make_async_copy(
@@ -289,7 +295,7 @@
 
     def await_grads():
         for z in range(line):
-            await_bytes(gz.at[:, z, pl.ds(0, dps - 1)], ogd_recv.at[z])
+            await_bytes(gz.at[z, pl.ds(0, dps - 1)], ogd_recv.at[z])
 
     depth = LAG * (line - 1)
 
@@ -303,7 +309,7 @@
         def _():
             await_grads()
 
-        when_chunk(t - BEHIND, lambda k: await_bytes(qw.at[other, k], qw_recv.at[k]))
+        when_chunk(t - BEHIND, lambda k: await_bytes(qw_of(k, other), qw_recv.at[k]))
         when_chunk(t - BEHIND - LAG * me, sum_right)
         when_chunk(t - BEHIND - LAG * (line - 1 - me), sum_left)
 
@@ -336,16 +342,16 @@
 
     await_bytes(stp.at[pl.ds(0, dps - 1)], st_send)
     await_bytes(slot_all.at[pl.ds(0, dps - 1)], slot_send)
-    await_bytes(gz.at[:, pl.ds(0, line - 1), 0], ogz_send)
-    await_bytes(gz.at[:, :, pl.ds(0, dps - 1)], ogd_send)
+    await_bytes(gz.at[pl.ds(0, line - 1), 0], ogz_send)
+    await_bytes(gz.at[:, pl.ds(0, dps - 1)], ogd_send)
     await_bytes(inc.at[:, pl.ds(0, dps - 1)], inc_send)
-    await_bytes(qw.at[0], qw_send)
+    await_bytes(gs, qw_send)
     await_bytes(gs, gr_send)
     await_bytes(rr.at[:, pl.ds(0, line - 1)], rs_send)
 
     @pl.when((me == 0) | (me == line - 1))
     def _():
-        await_bytes(acts.at[:, 0], ag_send)
+        await_bytes(rr.at[:, 0], ag_send)
 
     @pl.when((me > 0) & (me < line - 1))
     def _():
@@ -363,15 +369,23 @@
     hidden = features // dps
     own_rows, all_columns = out_grads.shape
     rows = own_rows * dps
-    cols = latent_weight.shape[1]
+    true_cols = latent_weight.shape[1]
     K = min(CHUNKS, hidden // 128)
     width = hidden // K
-    grads = out_grads.reshape(own_rows, line, 2, cols).transpose(1, 2, 0, 3)
+    spare = -true_cols % 128
+    cols = true_cols + spare
+    grads = out_grads
+    if spare:
+        grads = jnp.pad(
+            out_grads.reshape(own_rows, 2 * line, true_cols), ((0, 0), (0, 0), (0, spare))
+        ).reshape(own_rows, 2 * line * cols)
+        latent_weight = jnp.pad(latent_weight, ((0, 0), (0, spare)))
+        step_size = jnp.pad(step_size, ((0, 0), (0, spare)), constant_values=1)
     bf16, f32 = jnp.bfloat16, jnp.float32
     vmem = pl.BlockSpec(memory_space=pltpu.VMEM)
     hbm = pl.BlockSpec(memory_space=pl.ANY)
     dma = pltpu.SemaphoreType.DMA
-    return pl.pallas_call(
+    grad_acts, grad_weight, grad_step = pl.pallas_call(
         functools.partial(kernel, line, dps),
         out_shape=(
             jax.ShapeDtypeStruct((cap, features), bf16),
@@ -384,16 +398,20 @@
             pltpu.VMEM((K, dps, cap, width), bf16),
             pltpu.VMEM((dps, 1, cap), jnp.int32),
             pltpu.VMEM((rows, dps * cap), bf16),
-            pltpu.VMEM((K, line, rows, width), bf16),
+            pltpu.VMEM((dps * cap, rows), bf16),
+            pltpu.VMEM((K, line, width, rows), bf16),
             pltpu.VMEM((K, rows, width), f32),
-            pltpu.VMEM((2, line, dps, own_rows, cols), bf16),
-            pltpu.VMEM((2, K, width, cols), bf16),
+            pltpu.VMEM((line, dps, own_rows, 2 * cols), bf16),
+            pltpu.VMEM((K, 2 * cols, width), bf16),
             pltpu.VMEM((K, line + 1, rows, width), bf16),
             pltpu.VMEM((K, width, cols), f32),
             pltpu.VMEM((K, width, cols), f32),
             pltpu.VMEM((K, width, cols), bf16),
             pltpu.VMEM((K, width, cols), bf16),
+            pltpu.VMEM((LAG + 1, width, cols), f32),
             pltpu.VMEM((rows, width), f32),
+            pltpu.VMEM((rows, width), bf16),
+            pltpu.VMEM((width, cols), bf16),
             pltpu.VMEM((dps, 1, cols), f32),
             dma, dma, dma((line,)), dma, dma((line,)), dma, dma((K,)), dma,
             dma((K,)), dma, dma((K, line)), dma, dma((K, line + 1)), dma, dma((K,)), dma,
@@ -407,6 +425,9 @@
             transcendentals=0,
         ),
     )(patch_acts, patch_slot.reshape(1, cap), grads, latent_weight.reshape(K, width, cols), step_size)
+    if spare:
+        grad_weight, grad_step = grad_weight[:, :true_cols], grad_step[:, :true_cols]
+    return grad_acts, grad_weight, grad_step
 
 
 def solution(mesh):

time: 188 us -> 186 us (0.989)
  local copies, waits for them, and re-layouts: 8.81 us -> 6.74 us
    reshape x2 -> x0, local copies, waits for them, and re-layouts: 2.07 us -> none  [shards(): grads = out_grads.reshape(own_rows, line, 2, cols).transpose(1, 2, 0, 3)]
where the time goes in v6:
time: 186 us
  Pallas kernels  178 us (96%)
  local copies, waits for them, and re-layouts  6.74 us (4%)
    pallas_call x1, Pallas kernels, shards(): pl.pallas_call(functools.partial(kernel, line, dps), out_shape=(jax.Shape...  178 us
    unnamed x7, local copies, waits for them, and re-layouts  6.74 us

profile of v6, /device:TPU:1, one launch (start us, length us, event | category | flops | bytes accessed | tf_op | source)
XLA Modules:
  0.0 185.9 jit_solution(13387607344898887743)
XLA Ops:
  0.6 178.5 %shard_map.76 = (bf16[128,12288]{1,0:T(8,128)(2,1)}, f32[3072,384]{1,0:T(8,128)}, f32[1,384]{1,0:T(1,128)}) custom-call(bf16[128,12288]{1,0:T(8,128)(2,1)} %acts_hbm.1, s32[1,128]{1,0:T(1,128)} %bitcast.3, bf16[64,3072]{1,0:T(8,128)(2,1)} %og_ref.1, bf16[12,256,384]{2,1,0:T(8,128)(2,1)} %bitcast.2, bf16[1,384]{1,0:T(2,128)(2,1)} %step_ref.1), custom_call_target="tpu_custom_call" | custom-call | flops 9663676416 | bytes 6291456 | tf_op jit(solution)/shard_map/pallas_call | solution.py:388
  179.1 0.0 copy-start
  179.1 4.0 %copy.11 = bf16[128,12288]{1,0:T(8,128)(2,1)} copy(bf16[128,12288]{1,0:T(8,128)(2,1)} %get-tuple-element.6) | data formatting | bytes 6291456
  183.1 0.0 copy-done
  183.1 0.0 copy-start.1
  183.1 2.2 %copy.12 = f32[3072,384]{1,0:T(8,128)} copy(f32[3072,384]{1,0:T(8,128)S(1)} %copy-done) | data formatting | bytes 9437184
  185.3 0.0 copy-done.1
  185.3 0.6 copy.13
Async XLA Ops:
  179.1 4.0 %copy-start = (f32[3072,384]{1,0:T(8,128)S(1)}, f32[3072,384]{1,0:T(8,128)}, u32[]{:S(2)}) copy-start(f32[3072,384]{1,0:T(8,128)} %get-tuple-element.7) | copy-start | bytes 14155780
  183.1 2.2 %copy-start.1 = (f32[1,384]{1,0:T(1,128)S(1)}, f32[1,384]{1,0:T(1,128)}, u32[]{:S(2)}) copy-start(f32[1,384]{1,0:T(1,128)} %get-tuple-element.8) | copy-start | bytes 4612

commit v7 on v6

--- a/solution.py
+++ b/solution.py
@@ -10,7 +10,7 @@
 FF_W = 12288
 CHUNKS = 12
 LAG = 1
-BEHIND = 2
+BEHIND = 3
 AHEAD = 4
 MESH = pl.DeviceIdType.MESH
 
@@ -61,7 +61,7 @@
     line, dps, acts_hbm, slots_ref, og_ref, latent_ref, step_ref,
     ga_hbm, gw_hbm, gstep_ref,
     inc, slot_all, place, picks, acts, gelu_slope, gz, qw, rr, sl, res, gs, gr, own, tmp, act, quant, stp,
-    slot_recv, slot_send, ogz_recv, ogz_send, ogd_recv, ogd_send, inc_recv, inc_send,
+    slot_recv, slot_send, ogz_recv, ogz_send, ogp_recv, ogd_recv, ogd_send, inc_recv, inc_send,
     qw_recv, qw_send, ag_recv, ag_send, rs_recv, rs_send, gr_recv, gr_send,
     ga_recv, ga_send, gw_sem, st_recv, st_send,
 ):
@@ -83,6 +83,8 @@
     right = at(jnp.minimum(me + 1, line - 1), side, d)
     left = at(jnp.maximum(me - 1, 0), side, d)
     mates = [lax.rem(d + j, dps) for j in range(1, dps)]
+    mate = d + 1 - 2 * lax.rem(d, 2)
+    peers = [lax.rem(d + 2 * j, dps) for j in range(1, dps // 2)]
     others = [lax.rem(me + j, line) for j in range(1, line)]
 
     def remote(src, dst, send, recv, device):
@@ -120,8 +122,16 @@
         pltpu.make_async_copy(src, inc.at[k, d], inc_recv.at[k]).start()
 
     def forward_grads(z):
-        for e in mates:
-            remote(gz.at[z, d], gz.at[z, d], ogd_send, ogd_recv.at[z], at(me, side, e)).start()
+        block = gz.at[z, d]
+        for e in peers:
+            remote(block, block, ogd_send, ogp_recv.at[z], at(me, side, e)).start()
+        remote(block, block, ogd_send, ogd_recv.at[z], at(me, side, mate)).start()
+
+    def relay_grads(z):
+        await_bytes(gz.at[z, pl.ds(0, dps // 2 - 1)], ogp_recv.at[z])
+        for e in peers:
+            block = gz.at[z, e]
+            remote(block, block, ogd_send, ogd_recv.at[z], at(me, side, mate)).start()
 
     step = step_ref[...].astype(jnp.float32)
     inv_step = 1.0 / step
@@ -295,12 +305,17 @@
 
     def await_grads():
         for z in range(line):
-            await_bytes(gz.at[z, pl.ds(0, dps - 1)], ogd_recv.at[z])
+            await_bytes(gz.at[z, pl.ds(0, dps // 2)], ogd_recv.at[z])
 
     depth = LAG * (line - 1)
 
     def turn(t, carry):
         when_chunk(t, pack)
+
+        @pl.when(t == 1)
+        def _():
+            for z in range(line):
+                relay_grads(z)
 
         for h in range(1, line):
             when_chunk(t - LAG * h, lambda k, h=h: hop(k, h))
@@ -413,7 +428,7 @@
             pltpu.VMEM((rows, width), bf16),
             pltpu.VMEM((width, cols), bf16),
             pltpu.VMEM((dps, 1, cols), f32),
-            dma, dma, dma((line,)), dma, dma((line,)), dma, dma((K,)), dma,
+            dma, dma, dma((line,)), dma, dma((line,)), dma((line,)), dma, dma((K,)), dma,
             dma((K,)), dma, dma((K, line)), dma, dma((K, line + 1)), dma, dma((K,)), dma,
             dma, dma, dma, dma, dma,
         ],

time: 186 us -> 184 us (0.989)
    pallas_call x1, Pallas kernels: 178 us -> 177 us  [shards(): pl.pallas_call(functools.partial(kernel, line, dps), out_shape=(jax.Shape...]
where the time goes in v7:
time: 184 us
  Pallas kernels  177 us (96%)
  local copies, waits for them, and re-layouts  6.74 us (4%)
    pallas_call x1, Pallas kernels, shards(): pl.pallas_call(functools.partial(kernel, line, dps), out_shape=(jax.Shape...  177 us
    unnamed x7, local copies, waits for them, and re-layouts  6.74 us

profile of v7, /device:TPU:1, one launch (start us, length us, event | category | flops | bytes accessed | tf_op | source)
XLA Modules:
  0.0 184.0 jit_solution(9892077011175107610)
XLA Ops:
  0.6 176.6 %shard_map.76 = (bf16[128,12288]{1,0:T(8,128)(2,1)}, f32[3072,384]{1,0:T(8,128)}, f32[1,384]{1,0:T(1,128)}) custom-call(bf16[128,12288]{1,0:T(8,128)(2,1)} %acts_hbm.1, s32[1,128]{1,0:T(1,128)} %bitcast.3, bf16[64,3072]{1,0:T(8,128)(2,1)} %og_ref.1, bf16[12,256,384]{2,1,0:T(8,128)(2,1)} %bitcast.2, bf16[1,384]{1,0:T(2,128)(2,1)} %step_ref.1), custom_call_target="tpu_custom_call" | custom-call | flops 9663676416 | bytes 6291456 | tf_op jit(solution)/shard_map/pallas_call | solution.py:403
  177.3 0.0 copy-start
  177.3 4.0 %copy.11 = bf16[128,12288]{1,0:T(8,128)(2,1)} copy(bf16[128,12288]{1,0:T(8,128)(2,1)} %get-tuple-element.6) | data formatting | bytes 6291456
  181.3 0.0 copy-done
  181.3 0.0 copy-start.1
  181.3 2.2 %copy.12 = f32[3072,384]{1,0:T(8,128)} copy(f32[3072,384]{1,0:T(8,128)S(1)} %copy-done) | data formatting | bytes 9437184
  183.4 0.0 copy-done.1
  183.5 0.6 copy.13
Async XLA Ops:
  177.3 4.0 %copy-start = (f32[3072,384]{1,0:T(8,128)S(1)}, f32[3072,384]{1,0:T(8,128)}, u32[]{:S(2)}) copy-start(f32[3072,384]{1,0:T(8,128)} %get-tuple-element.7) | copy-start | bytes 14155780
  181.3 2.2 %copy-start.1 = (f32[1,384]{1,0:T(1,128)S(1)}, f32[1,384]{1,0:T(1,128)}, u32[]{:S(2)}) copy-start(f32[1,384]{1,0:T(1,128)} %get-tuple-element.8) | copy-start | bytes 4612

commit v8 on v7

--- a/solution.py
+++ b/solution.py
@@ -223,6 +223,7 @@
             @pl.when(me + j <= line - 1)
             def _():
                 z = me + j
+                part = partial_hidden(z, k)
 
                 @pl.when(me > 0)
                 def _():
@@ -232,7 +233,7 @@
                 def _():
                     clear(k, z)
 
-                total = rr[k, z].astype(jnp.float32) + partial_hidden(z, k)
+                total = rr[k, z].astype(jnp.float32) + part
                 rr[k, z] = total.astype(jnp.bfloat16)
                 remote(rr.at[k, z], rr.at[k, z], rs_send, rs_recv.at[k, z], right).start()
 
@@ -242,6 +243,7 @@
             def _():
                 z = me - j
                 slot = line if j == 1 else z
+                part = partial_hidden(z, k)
 
                 @pl.when(me < line - 1)
                 def _():
@@ -251,11 +253,13 @@
                 def _():
                     clear(k, z)
 
-                total = rr[k, z].astype(jnp.float32) + partial_hidden(z, k)
+                total = rr[k, z].astype(jnp.float32) + part
                 rr[k, z] = total.astype(jnp.bfloat16)
                 remote(rr.at[k, z], rr.at[k, slot], rs_send, rs_recv.at[k, slot], left).start()
 
     def finish_hidden(k):
+        part = partial_hidden(me, k)
+
         @pl.when(me > 0)
         def _():
             await_bytes(rr.at[k, me], rs_recv.at[k, me])
@@ -272,7 +276,7 @@
         def _():
             clear(k, line)
 
-        total = rr[k, me].astype(jnp.float32) + rr[k, line].astype(jnp.float32) + partial_hidden(me, k)
+        total = rr[k, me].astype(jnp.float32) + rr[k, line].astype(jnp.float32) + part
         packed = (total * gelu_slope[k]).astype(jnp.bfloat16)
         picked = dot(picks[...], packed, 1, 0).astype(jnp.bfloat16)
         inc[k] = picked.reshape(dps, cap, width)

time: 184 us -> 184 us (level)
  no operation moved by 1% of the time
where the time goes in v8:
time: 184 us
  Pallas kernels  176 us (96%)
  local copies, waits for them, and re-layouts  6.74 us (4%)
    pallas_call x1, Pallas kernels, shards(): pl.pallas_call(functools.partial(kernel, line, dps), out_shape=(jax.Shape...  176 us
    unnamed x7, local copies, waits for them, and re-layouts  6.74 us

profile of v8, /device:TPU:1, one launch (start us, length us, event | category | flops | bytes accessed | tf_op | source)
XLA Modules:
  0.0 183.6 jit_solution(1517783181115041915)
XLA Ops:
  0.6 176.2 %shard_map.76 = (bf16[128,12288]{1,0:T(8,128)(2,1)}, f32[3072,384]{1,0:T(8,128)}, f32[1,384]{1,0:T(1,128)}) custom-call(bf16[128,12288]{1,0:T(8,128)(2,1)} %acts_hbm.1, s32[1,128]{1,0:T(1,128)} %bitcast.3, bf16[64,3072]{1,0:T(8,128)(2,1)} %og_ref.1, bf16[12,256,384]{2,1,0:T(8,128)(2,1)} %bitcast.2, bf16[1,384]{1,0:T(2,128)(2,1)} %step_ref.1), custom_call_target="tpu_custom_call" | custom-call | flops 9663676416 | bytes 6291456 | tf_op jit(solution)/shard_map/pallas_call | solution.py:407
  176.9 0.0 copy-start
  176.9 4.0 %copy.11 = bf16[128,12288]{1,0:T(8,128)(2,1)} copy(bf16[128,12288]{1,0:T(8,128)(2,1)} %get-tuple-element.6) | data formatting | bytes 6291456
  180.9 0.0 copy-done
  180.9 0.0 copy-start.1
  180.9 2.2 %copy.12 = f32[3072,384]{1,0:T(8,128)} copy(f32[3072,384]{1,0:T(8,128)S(1)} %copy-done) | data formatting | bytes 9437184
  183.1 0.0 copy-done.1
  183.1 0.6 copy.13
Async XLA Ops:
  176.9 4.0 %copy-start = (f32[3072,384]{1,0:T(8,128)S(1)}, f32[3072,384]{1,0:T(8,128)}, u32[]{:S(2)}) copy-start(f32[3072,384]{1,0:T(8,128)} %get-tuple-element.7) | copy-start | bytes 14155780
  180.9 2.2 %copy-start.1 = (f32[1,384]{1,0:T(1,128)S(1)}, f32[1,384]{1,0:T(1,128)}, u32[]{:S(2)}) copy-start(f32[1,384]{1,0:T(1,128)} %get-tuple-element.8) | copy-start | bytes 4612
